TPU v7x, 32 devices: a whole 2x2x4 slice. The times are simulated.
32 devices in a mesh: band: 8 (over z, x), domain: 4 (over y, core).
Axes of the slice: x: 2, y: 2, z: 4, core: 2. Of those that a mesh axis runs over, the one named last changes fastest.
Arguments:
- orbitals: float32 [256, 4096], P('band', 'domain'), may hold values from -12 to 12
- potential: float32 [4096], P('domain'), may hold values from -9 to 4.5
- stencil: int32 [36, 4096], P(None, 'domain'), may hold values from 0 to 1536, as said below
- send_list: int32 [2, 1024], P(None, 'domain'), may hold values from 0 to 1023, as said below
- send_count: int32 [2, 4], P(None, 'domain'), may hold values from 0 to 256, as said below
Outputs:
- filtered: float32 [256, 4096], P('band', 'domain')
- correlation: float32 [256, 256], P('band', 'domain')
- subspace: float32 [256, 256], P('band', 'domain')
Inputs may be any that keep to these rules, and one draw needn't show every extreme that they name: `stencil`: entries below 1024 name a slot of the point's own subdomain; entries from 1024 on name only live boundary rows of an existing neighbouring subdomain; 1536 marks a neighbour outside the cluster. `send_list`: each list of 256 entries holds distinct slots of the sending subdomain. `send_count`: row 0 counts the rows subdomain d sends to d + 1, row 1 those it sends to d - 1; zero toward a missing neighbour; 256 is reached in every draw.
All inputs are finite; a program needn't handle non-finite values.
Results may differ from a plain program's by a relative error of at most 0.00015.
Values sent between devices are 32-bit elements; how exact they have to be, the bound alone decides.
A program may use at most 128 MiB of HBM per device.

v0:
```python
import jax
import jax.numpy as jnp
from jax import lax
from jax.sharding import PartitionSpec as P

DEGREE = 4


WEIGHTS = (
    -5369.0 / 1800.0,
    12.0 / 7.0,
    -15.0 / 56.0,
    10.0 / 189.0,
    -1.0 / 112.0,
    2.0 / 1925.0,
    -1.0 / 16632.0,
)
KINETIC = 50.0 / 9.0
CUT_SHARE = 0.1
SPECTRAL_REACH = (
    KINETIC
    * 3.0
    * (
        abs(WEIGHTS[0])
        + 2.0
        * (
            abs(WEIGHTS[1])
            + abs(WEIGHTS[2])
            + abs(WEIGHTS[3])
            + abs(WEIGHTS[4])
            + abs(WEIGHTS[5])
            + abs(WEIGHTS[6])
        )
    )
)


def with_halo(block, sides, width):
    for axis, dim in sides:
        count = lax.axis_size(axis)
        forward = [(i, i + 1) for i in range(count - 1)]
        backward = [(target, source) for source, target in forward]
        low = lax.ppermute(
            lax.slice_in_dim(block, block.shape[dim] - width, None, axis=dim), axis, forward
        )
        high = lax.ppermute(lax.slice_in_dim(block, 0, width, axis=dim), axis, backward)
        block = jnp.concatenate([low, block, high], axis=dim)
    return block


def apply_operator(values, potential, stencil, send_list, live_slots):
    capacity = send_list.shape[1]
    sent_rows = values[:, send_list]
    sent_rows = jnp.where(live_slots[None], sent_rows, jnp.zeros_like(sent_rows))
    outgoing = jnp.concatenate([sent_rows[:, 1], sent_rows[:, 0]], axis=1)
    padded = with_halo(outgoing, (("domain", 1),), capacity)
    from_below = padded[:, :capacity]
    from_above = padded[:, 3 * capacity :]
    zero_column = jnp.zeros((values.shape[0], 1), values.dtype)
    buffer = jnp.concatenate([values, from_below, from_above, zero_column], axis=1)
    near_sum = jnp.zeros_like(values)
    for distance in range(6):
        cycle_sum = jnp.zeros_like(values)
        for member in range(6):
            cycle_sum = cycle_sum + buffer[:, stencil[6 * distance + member]]
        near_sum = near_sum + WEIGHTS[distance + 1] * cycle_sum
    return potential * values - KINETIC * (3.0 * WEIGHTS[0] * values + near_sum)


def filter_block(orbitals, operator_fn, lowest, highest):
    top_bound = highest + SPECTRAL_REACH
    cut_point = lowest + CUT_SHARE * (top_bound - lowest)
    half_width = (top_bound - cut_point) / 2.0
    centre = (top_bound + cut_point) / 2.0
    sigma_now = half_width / (lowest - centre)
    sigma_scale = 2.0 / sigma_now
    previous = orbitals
    current = sigma_now / half_width * (operator_fn(orbitals) - centre * orbitals)
    for order_index in range(2, DEGREE + 1):
        sigma_next = 1.0 / (sigma_scale - sigma_now)
        following = (
            2.0 * sigma_next / half_width * (operator_fn(current) - centre * current)
            - sigma_now * sigma_next * previous
        )
        previous = current
        current = following
        sigma_now = sigma_next
    return current


def inner_products(left_block, right_block):
    return lax.dot_general(
        left_block,
        right_block,
        (((1,), (1,)), ((), ())),
        precision=lax.Precision.HIGHEST,
        preferred_element_type=jnp.float32,
    )


def shards(orbitals, potential, stencil, send_list, send_count):
    points = orbitals.shape[1]
    capacity = send_list.shape[1]
    domain_count = lax.axis_size("domain")
    total_points = points * domain_count
    lowest = lax.pmin(jnp.min(potential), "domain")
    highest = lax.pmax(jnp.max(potential), "domain")
    live_slots = lax.broadcasted_iota(jnp.int32, (2, capacity), 1) < send_count

    def operator_fn(values):
        return apply_operator(values, potential, stencil, send_list, live_slots)

    filtered = filter_block(orbitals, operator_fn, lowest, highest)
    applied = operator_fn(filtered)
    piece_values = lax.all_gather(filtered, "band", axis=0, tiled=True)
    piece_applied = lax.all_gather(applied, "band", axis=0, tiled=True)
    correlation_part = inner_products(filtered, piece_values)
    subspace_part = inner_products(filtered, piece_applied)
    correlation_part, subspace_part = (correlation_part, subspace_part)
    correlation_sum, subspace_sum = (
        lax.psum_scatter(correlation_part, "domain", scatter_dimension=1, tiled=True),
        lax.psum_scatter(subspace_part, "domain", scatter_dimension=1, tiled=True),
    )
    return (filtered, correlation_sum / total_points, subspace_sum / total_points)


def solution(mesh):
    placed = (
        P("band", "domain"),
        P("domain"),
        P(None, "domain"),
        P(None, "domain"),
        P(None, "domain"),
    )
    return jax.shard_map(
        shards,
        mesh=mesh,
        in_specs=placed,
        out_specs=(P("band", "domain"), P("band", "domain"), P("band", "domain")),
        check_vma=False,
    )
```

profile of v0, /device:TPU:0, one launch (start us, length us, event | category | flops | bytes accessed | tf_op | source)
XLA Modules:
  0.0 1036.2 jit_solution(15216150083317706961)
XLA Ops:
  17.4 9.5 pmax.7
  26.9 7.4 pmin.7
  171.2 4.0 gather_fusion.39
  199.2 4.0 gather_fusion.60
  211.2 4.0 gather_fusion.63
  247.2 4.0 gather_fusion.38
  365.2 4.5 collective-permute-start.4
  373.2 4.0 gather_fusion.76
  401.1 4.0 gather_fusion.97
  413.1 4.0 gather_fusion.100
  449.2 4.0 gather_fusion.75
  566.5 4.0 collective-permute-start.6
  573.9 4.0 gather_fusion.113
  601.9 4.0 gather_fusion.134
  613.9 4.0 gather_fusion.137
  649.9 4.0 gather_fusion.112
  768.3 4.0 collective-permute-start.8
  790.0 4.0 gather_fusion.169
  830.0 4.0 gather_fusion.179
  854.0 4.0 gather_fusion.152
  870.0 4.0 gather_fusion.156
  945.2 39.8 %all-gather.5.cloned.1.call-done = f32[256,1024]{1,0:T(8,128)} async-done(((f32[32,1024]{1,0:T(8,128)}), f32[256,1024]{1,0:T(8,128)}) %all-gather.5.cloned.1.call-update) | async-done | bytes 1048592 | tf_op jit(solution)/shard_map/all_gather | solution.py:116
  987.9 17.9 %reduce-scatter.7.cloned.1.call-done = f32[64,32]{1,0:T(8,128)} async-done(((f32[256,32]{1,0:T(8,128)}), f32[64,32]{1,0:T(8,128)}) %reduce-scatter.7.cloned.1.call-update) | async-done | bytes 8208
  1007.3 20.6 %reduce-scatter.9.cloned.1.call-done = f32[64,32]{1,0:T(8,128)} async-done(((f32[256,32]{1,0:T(8,128)}), f32[64,32]{1,0:T(8,128)}) %reduce-scatter.9.cloned.1.call-update) | async-done | bytes 8208
  (1071 shorter events, 844.7 us)
Async XLA Ops:
  7.2 935.1 %all-gather.3.cloned.1.call-start = ((), (), s32[]{:S(2)}) async-start(), calls=%async_computation.2 | async-start | bytes 1179648 | tf_op jit(solution)/shard_map/all_gather | solution.py:115
  11.4 25.5 %collective-permute-start = (f32[32,256]{1,0:T(8,128)S(1)}, f32[32,256]{1,0:T(8,128)S(1)}, u32[]{:S(2)}, u32[]{:S(2)}) collective-permute-start(f32[32,256]{1,0:T(8,128)S(1)} %get-tuple-element.64), channel_id=1, source_target_pairs={{0,1},{1,2},{2,3},{4,5},{5,6},{6,7},{8,9},{9,10},{10,11},{12,13},{... | collective-permute-start | bytes 98312 | tf_op jit(solution)/shard_map/ppermute | solution.py:43
  13.8 23.3 %collective-permute-start.1 = (f32[32,256]{1,0:T(8,128)S(1)}, f32[32,256]{1,0:T(8,128)S(1)}, u32[]{:S(2)}, u32[]{:S(2)}) collective-permute-start(f32[32,256]{1,0:T(8,128)S(1)} %get-tuple-element.65), channel_id=1, source_target_pairs={{1,0},{2,1},{3,2},{5,4},{6,5},{7,6},{9,8},{10,9},{11,10},{13,12},{... | collective-permute-start | bytes 98312 | tf_op jit(solution)/shard_map/ppermute | solution.py:46
  15.8 104.2 %copy-start.234 = (s32[1024]{0:T(1024)}, s32[1024]{0:T(1024)S(1)}, u32[]{:S(2)}) copy-start(s32[1024]{0:T(1024)S(1)} %broadcast_clamp_fusion.28) | copy-start | bytes 12292
  15.9 107.8 %copy-start.239 = (s32[1024]{0:T(1024)}, s32[1024]{0:T(1024)S(1)}, u32[]{:S(2)}) copy-start(s32[1024]{0:T(1024)S(1)} %broadcast_clamp_fusion.27) | copy-start | bytes 12292
  15.9 111.4 %copy-start.244 = (s32[1024]{0:T(1024)}, s32[1024]{0:T(1024)S(1)}, u32[]{:S(2)}) copy-start(s32[1024]{0:T(1024)S(1)} %broadcast_clamp_fusion.26) | copy-start | bytes 12292
  15.9 115.0 %copy-start.249 = (s32[1024]{0:T(1024)}, s32[1024]{0:T(1024)S(1)}, u32[]{:S(2)}) copy-start(s32[1024]{0:T(1024)S(1)} %broadcast_clamp_fusion.25) | copy-start | bytes 12292
  15.9 118.6 %copy-start.254 = (s32[1024]{0:T(1024)}, s32[1024]{0:T(1024)S(1)}, u32[]{:S(2)}) copy-start(s32[1024]{0:T(1024)S(1)} %broadcast_clamp_fusion.24) | copy-start | bytes 12292
  16.0 122.3 %copy-start.259 = (s32[1024]{0:T(1024)}, s32[1024]{0:T(1024)S(1)}, u32[]{:S(2)}) copy-start(s32[1024]{0:T(1024)S(1)} %broadcast_clamp_fusion.23) | copy-start | bytes 12292
  16.0 125.9 %copy-start.264 = (s32[1024]{0:T(1024)}, s32[1024]{0:T(1024)S(1)}, u32[]{:S(2)}) copy-start(s32[1024]{0:T(1024)S(1)} %broadcast_clamp_fusion.22) | copy-start | bytes 12292
  16.0 129.5 %copy-start.269 = (s32[1024]{0:T(1024)}, s32[1024]{0:T(1024)S(1)}, u32[]{:S(2)}) copy-start(s32[1024]{0:T(1024)S(1)} %broadcast_clamp_fusion.21) | copy-start | bytes 12292
  16.0 133.1 %copy-start.274 = (s32[1024]{0:T(1024)}, s32[1024]{0:T(1024)S(1)}, u32[]{:S(2)}) copy-start(s32[1024]{0:T(1024)S(1)} %broadcast_clamp_fusion.20) | copy-start | bytes 12292
  16.0 136.8 %copy-start.279 = (s32[1024]{0:T(1024)}, s32[1024]{0:T(1024)S(1)}, u32[]{:S(2)}) copy-start(s32[1024]{0:T(1024)S(1)} %broadcast_clamp_fusion.1) | copy-start | bytes 12292
  165.6 3.2 collective-permute-start.2
  166.9 4.1 collective-permute-start.3
  365.2 6.1 collective-permute-start.4
  369.8 3.1 collective-permute-start.5
  566.5 5.7 collective-permute-start.6
  570.5 3.1 collective-permute-start.7
  765.5 219.5 %all-gather.5.cloned.1.call-start = ((), (), s32[]{:S(2)}) async-start(), calls=%async_computation.3 | async-start | bytes 1179648 | tf_op jit(solution)/shard_map/all_gather | solution.py:116
  768.3 5.6 collective-permute-start.8
  772.3 3.1 collective-permute-start.9
  942.2 63.6 %reduce-scatter.7.cloned.1.call-start = ((), (), s32[]{:S(2)}) async-start(), calls=%async_computation.4 | async-start | bytes 163840
  945.2 82.7 %reduce-scatter.9.cloned.1.call-start = ((), (), s32[]{:S(2)}) async-start(), calls=%async_computation.5 | async-start | bytes 163840
  (295 other events, 2250.7 us)
Sparse Core Ops, SparseCore 0:
  765.6 42.2 all-gather.2
  942.4 42.6 all-gather.4
  987.5 18.3 reduce-scatter.6
  1008.2 19.5 reduce-scatter.8
where the time goes:
time: 1050 us; the launch traced here: 1040 us
  local copies, waits for them, and re-layouts  869 us (83%)
  waiting for transfers between devices  85.1 us (8%)
  starting transfers between devices  24 us (2%)
  between operations  19.5 us (2%)
  blocking collectives  16.9 us (2%)
  other arithmetic  16.3 us (2%)
    gather x360, local copies, waits for them, and re-layouts, apply_operator(): cycle_sum = cycle_sum + buffer[:, stencil[6 * distance + member]]  843 us
    all_gather x1, waiting for transfers between devices, shards(): piece_applied = lax.all_gather(applied, 'band', axis=0, tiled=True)  39.8 us
    unnamed x6, waiting for transfers between devices  38.5 us
  transfers between devices with their start and end apart: 14, of which 7 were waited for; matrix products, arithmetic and copies ran while one was open for 17% of the time, Pallas kernels for 0%

commit v1 on v0

v1 whole, which is shorter than its diff:
```python
import functools

import jax
import jax.numpy as jnp
from jax import lax
from jax.experimental import pallas as pl
from jax.experimental.pallas import tpu as pltpu
from jax.sharding import PartitionSpec as P

DEGREE = 4
WEIGHTS = (
    -5369.0 / 1800.0,
    12.0 / 7.0,
    -15.0 / 56.0,
    10.0 / 189.0,
    -1.0 / 112.0,
    2.0 / 1925.0,
    -1.0 / 16632.0,
)
KINETIC = 50.0 / 9.0
CUT_SHARE = 0.1
SPECTRAL_REACH = KINETIC * 3.0 * (abs(WEIGHTS[0]) + 2.0 * sum(abs(w) for w in WEIGHTS[1:]))
MESH = pl.DeviceIdType.MESH
DIGITS = 8
f32, bf16, i32 = jnp.float32, jnp.bfloat16, jnp.int32


def remote(src, dst, send_sem, recv_sem, device_id):
    return pltpu.make_async_remote_copy(
        src_ref=src,
        dst_ref=dst,
        send_sem=send_sem,
        recv_sem=recv_sem,
        device_id=device_id,
        device_id_type=MESH,
    )


def split(x):
    hi = x.astype(bf16)
    lo = (x - hi.astype(f32)).astype(bf16)
    return hi, lo


def dot3(stacked, hi_rows, right_hi, right_lo):
    both = jnp.dot(stacked, right_hi, preferred_element_type=f32)
    low = jnp.dot(stacked[:hi_rows], right_lo, preferred_element_type=f32)
    return both[:hi_rows] + both[hi_rows:] + low


def kernel(D, B, gram, orb_ref, pot_ref, sten_ref, list_ref, count_ref, filt_ref, out_ref, *scratch):
    ah, al, sel, slot, unit, mm, sent, halo, mm_ss, mm_rs, h_ss, h_rs = scratch[:12]
    d = lax.axis_index("domain")
    b = lax.axis_index("band")
    R, N = orb_ref.shape
    cap = list_ref.shape[1]
    groups = (N + 2 * cap) // DIGITS

    halo[...] = jnp.zeros_like(halo)
    barrier = pltpu.get_barrier_semaphore()
    for o in range(1, D):
        pl.semaphore_signal(
            barrier, inc=1, device_id={"domain": lax.rem(d + o, D)}, device_id_type=MESH
        )
    if gram:
        for o in range(1, B):
            pl.semaphore_signal(
                barrier, inc=1, device_id={"band": lax.rem(b + o, B)}, device_id_type=MESH
            )

    pot = pot_ref[...]
    mm[0, 0:1] = jnp.broadcast_to(jnp.min(pot, axis=1, keepdims=True), (1, 128))
    mm[0, 1:2] = jnp.broadcast_to(jnp.max(pot, axis=1, keepdims=True), (1, 128))
    live = lax.broadcasted_iota(i32, (2, cap), 1) < count_ref[...]
    lists = jnp.where(live, list_ref[...], -1)

    def sel_body(step, carry):
        start = pl.multiple_of(step * 128, 128)
        rows = lax.broadcasted_iota(i32, (128, cap), 0) + start
        for r in range(2):
            sel[pl.ds(start, 128), r * cap : (r + 1) * cap] = jnp.where(
                rows == lists[r : r + 1], 1.0, 0.0
            ).astype(bf16)
        return carry

    lax.fori_loop(0, N // 128, sel_body, 0)
    pl.semaphore_wait(barrier, (D - 1) + (B - 1 if gram else 0))

    mm_copies = []
    for o in range(1, D):
        copy = remote(
            mm.at[0], mm.at[o], mm_ss.at[o - 1], mm_rs.at[o - 1], {"domain": lax.rem(d + o, D)}
        )
        copy.start()
        mm_copies.append(copy)

    up = lax.rem(d + 1, D)
    down = lax.rem(d + D - 1, D)

    def halo_copies(step):
        return (
            remote(sent.at[step, 0], halo.at[step, 0], h_ss.at[step, 0], h_rs.at[step, 0], {"domain": up}),
            remote(sent.at[step, 1], halo.at[step, 1], h_ss.at[step, 1], h_rs.at[step, 1], {"domain": down}),
        )

    def send_halo(step, stacked):
        both = jnp.dot(stacked, sel[...], preferred_element_type=f32)
        rows = both[:R] + both[R:]
        sent[step, 0] = rows[:, :cap]
        sent[step, 1] = rows[:, cap:]
        upward, downward = halo_copies(step)
        pl.when(d < D - 1)(upward.start)
        pl.when(d > 0)(downward.start)

    def recv_halo(step):
        upward, downward = halo_copies(step)
        pl.when(d > 0)(upward.wait_recv)
        pl.when(d < D - 1)(downward.wait_recv)
        return jnp.concatenate([halo[step, 0], halo[step, 1]], axis=1)

    def done_halo(step):
        upward, downward = halo_copies(step)
        pl.when(d < D - 1)(upward.wait_send)
        pl.when(d > 0)(downward.wait_send)

    first = jnp.concatenate(split(orb_ref[...]), axis=0)
    send_halo(0, first)

    key = sten_ref[...]
    digit = (key * ((1 << 22) // groups + 1)) >> 22
    slot[...] = key - digit * groups
    unit[...] = jnp.where(digit < DIGITS, jnp.left_shift(1, 4 * jnp.minimum(digit, DIGITS - 1)), 0)

    chunk = 32

    def build(index, carry):
        lane = pl.multiple_of((index % (N // 128)) * 128, 128)
        row = pl.multiple_of((index // (N // 128)) * chunk, chunk)
        rows = lax.broadcasted_iota(i32, (chunk, 128), 0) + row
        acc = [jnp.zeros((chunk, 128), f32) for _ in range(DIGITS)]
        for j in range(6):
            word = jnp.zeros((chunk, 128), i32)
            for i in range(6 * j, 6 * j + 6):
                s = slot[i : i + 1, pl.ds(lane, 128)]
                u = unit[i : i + 1, pl.ds(lane, 128)]
                word = word + jnp.where(rows == s, u, 0)
            for r in range(DIGITS):
                count = (word & (7 << (4 * r))).astype(f32)
                acc[r] = acc[r] + count * (WEIGHTS[j + 1] / WEIGHTS[1] * 2.0 ** (-4 * r))
        for r in range(DIGITS):
            hi, lo = split(acc[r])
            ah[pl.ds(r * groups + row, chunk), pl.ds(lane, 128)] = hi
            al[pl.ds(r * groups + row, chunk), pl.ds(lane, 128)] = lo
        return carry

    lax.fori_loop(0, (N // 128) * (groups // chunk), build, 0)

    for copy in mm_copies:
        copy.wait()
    lowest = mm[0, 0:1, 0:1]
    highest = mm[0, 1:2, 0:1]
    for o in range(1, D):
        lowest = jnp.minimum(lowest, mm[o, 0:1, 0:1])
        highest = jnp.maximum(highest, mm[o, 1:2, 0:1])
    top = highest + SPECTRAL_REACH
    cut = lowest + CUT_SHARE * (top - lowest)
    half_width = (top - cut) / 2.0
    centre = (top + cut) / 2.0
    diagonal = pot - KINETIC * 3.0 * WEIGHTS[0]

    def near(step, stacked):
        total = dot3(stacked, R, ah[:N], al[:N])
        outer = jnp.concatenate(split(recv_halo(step)), axis=0)
        return WEIGHTS[1] * (total + dot3(outer, R, ah[N:], al[N:]))

    sigma = half_width / (lowest - centre)
    scale = 2.0 / sigma
    previous = orb_ref[...]
    factor = sigma / half_width
    current = factor * ((diagonal - centre) * previous - KINETIC * near(0, first))
    for j in range(2, DEGREE + 1):
        stacked = jnp.concatenate(split(current), axis=0)
        send_halo(j - 1, stacked)
        sigma_next = 1.0 / (scale - sigma)
        factor = 2.0 * sigma_next / half_width
        part_two = factor * (diagonal - centre) * current - (sigma * sigma_next) * previous
        following = part_two - (factor * KINETIC) * near(j - 1, stacked)
        previous, current, sigma = current, following, sigma_next
    filt_ref[...] = current
    stacked = jnp.concatenate(split(current), axis=0)
    send_halo(DEGREE, stacked)

    if not gram:
        out_ref[...] = diagonal * current - KINETIC * near(DEGREE, stacked)
        for step in range(DEGREE + 1):
            done_halo(step)
        return

    app, fall, aall, give, core_in, y_in, band_out, band_in = scratch[12:20]
    f_ss, f_rs, a_ss, a_rs, c_ss, c_rs, y_ss, y_rs, b_ss, b_rs = scratch[20:]
    wide = N // B

    def spread(src, dst, ss, rs):
        copies = []
        for o in range(1, B):
            to = lax.rem(b + o, B)
            copy = remote(
                src.at[:, pl.ds(pl.multiple_of(to * wide, wide), wide)],
                dst.at[b],
                ss.at[o - 1],
                rs.at[o - 1],
                {"band": to},
            )
            copy.start()
            copies.append(copy)
        dst[b] = src[:, pl.ds(pl.multiple_of(b * wide, wide), wide)]
        return copies

    f_copies = spread(filt_ref, fall, f_ss, f_rs)
    app[...] = diagonal * current - KINETIC * near(DEGREE, stacked)
    a_copies = spread(app, aall, a_ss, a_rs)
    for copy in f_copies:
        copy.wait_recv()
    orbs = B * R
    left = fall[...].reshape(orbs, wide)
    left_hi, left_lo = split(left)
    left_both = jnp.concatenate([left_hi, left_lo], axis=0)
    for copy in a_copies:
        copy.wait_recv()

    blocks = B // D
    core = lax.rem(d, 2)
    pair = d // 2
    rights = (((1,), (1,)), ((), ()))

    def partial(target):
        start = target * blocks
        right = jnp.concatenate(
            [
                fall[pl.ds(start, blocks)].reshape(blocks * R, wide),
                aall[pl.ds(start, blocks)].reshape(blocks * R, wide),
            ],
            axis=0,
        )
        right_hi, right_lo = split(right)
        both = lax.dot_general(left_both, right_hi, rights, preferred_element_type=f32)
        low = lax.dot_general(left_hi, right_lo, rights, preferred_element_type=f32)
        return both[:orbs] + both[orbs:] + low

    pairs = D // 2
    c_copies = []
    for q in range(pairs):
        turn = lax.rem(pair + 1 + q, pairs)
        give[q] = partial(2 * turn + (1 - core))
        copy = remote(
            give.at[q], core_in.at[q], c_ss.at[q], c_rs.at[q], {"domain": 2 * pair + 1 - core}
        )
        copy.start()
        c_copies.append(copy)
    y_copies = []
    for q in range(pairs):
        turn = lax.rem(pair + 1 + q, pairs)
        own = partial(2 * turn + core)
        c_copies[q].wait_recv()
        core_in[q] = core_in[q] + own
        if q < pairs - 1:
            copy = remote(
                core_in.at[q], y_in.at[q], y_ss.at[q], y_rs.at[q], {"domain": 2 * turn + core}
            )
            copy.start()
            y_copies.append(copy)
    total = core_in[pairs - 1]
    for q in range(pairs - 1):
        y_copies[q].wait_recv()
        total = total + y_in[q]
    band_out[...] = (total * (1.0 / (N * D))).reshape(band_out.shape)
    b_copies = []
    for o in range(1, B):
        to = lax.rem(b + o, B)
        copy = remote(band_out.at[to], band_in.at[o - 1], b_ss.at[o - 1], b_rs.at[o - 1], {"band": to})
        copy.start()
        b_copies.append(copy)
    result = band_out[b]
    for o in range(1, B):
        b_copies[o - 1].wait_recv()
        result = result + band_in[o - 1]
    out_ref[...] = result
    for step in range(DEGREE + 1):
        done_halo(step)
    for copy in f_copies + a_copies + c_copies + y_copies + b_copies:
        copy.wait_send()


def inner_products(left_block, right_block):
    return lax.dot_general(
        left_block,
        right_block,
        (((1,), (1,)), ((), ())),
        precision=lax.Precision.HIGHEST,
        preferred_element_type=f32,
    )


def shards(orbitals, potential, stencil, send_list, send_count):
    D, B = lax.axis_size("domain"), lax.axis_size("band")
    R, N = orbitals.shape
    cap = send_list.shape[1]
    orbs = R * B
    keys = N + 2 * cap
    gram = D == 4 and N % (128 * B) == 0 and B % D == 0 and 2 * orbs // D == 128
    steps = DEGREE + 1
    dma = pltpu.SemaphoreType.DMA
    scratch = [
        pltpu.VMEM((keys, N), bf16),
        pltpu.VMEM((keys, N), bf16),
        pltpu.VMEM((N, 2 * cap), bf16),
        pltpu.VMEM(stencil.shape, i32),
        pltpu.VMEM(stencil.shape, i32),
        pltpu.VMEM((D, 8, 128), f32),
        pltpu.VMEM((steps, 2, R, cap), f32),
        pltpu.VMEM((steps, 2, R, cap), f32),
        dma((D - 1,)),
        dma((D - 1,)),
        dma((steps, 2)),
        dma((steps, 2)),
    ]
    if gram:
        wide = N // B
        width = 2 * orbs // D
        pairs = D // 2
        scratch += [
            pltpu.VMEM((R, N), f32),
            pltpu.VMEM((B, R, wide), f32),
            pltpu.VMEM((B, R, wide), f32),
            pltpu.VMEM((pairs, orbs, width), f32),
            pltpu.VMEM((pairs, orbs, width), f32),
            pltpu.VMEM((pairs - 1, orbs, width), f32),
            pltpu.VMEM((B, R, width), f32),
            pltpu.VMEM((B - 1, R, width), f32),
        ]
        for count in (B - 1, B - 1, pairs, pairs - 1, B - 1):
            scratch += [dma((count,)), dma((count,))]
    second = (R, 2 * orbs // D) if gram else (R, N)
    filtered, other = pl.pallas_call(
        functools.partial(kernel, D, B, gram),
        out_shape=(
            jax.ShapeDtypeStruct((R, N), f32),
            jax.ShapeDtypeStruct(second, f32),
        ),
        in_specs=[pl.BlockSpec(memory_space=pltpu.VMEM)] * 5,
        out_specs=[pl.BlockSpec(memory_space=pltpu.VMEM)] * 2,
        scratch_shapes=scratch,
        compiler_params=pltpu.CompilerParams(
            collective_id=0, has_side_effects=True, vmem_limit_bytes=48 * 1024 * 1024
        ),
    )(orbitals, potential.reshape(1, N), stencil, send_list, send_count)
    if gram:
        half = orbs // D
        return filtered, other[:, :half], other[:, half:]
    results = []
    for block in (filtered, other):
        whole = lax.all_gather(block, "band", axis=0, tiled=True)
        share = inner_products(filtered, whole)
        total = lax.psum_scatter(share, "domain", scatter_dimension=1, tiled=True)
        results.append(total / (N * D))
    return filtered, results[0], results[1]


def solution(mesh):
    placed = (
        P("band", "domain"),
        P("domain"),
        P(None, "domain"),
        P(None, "domain"),
        P(None, "domain"),
    )
    return jax.shard_map(
        shards,
        mesh=mesh,
        in_specs=placed,
        out_specs=(P("band", "domain"), P("band", "domain"), P("band", "domain")),
        check_vma=False,
    )
```

time: 1050 us -> 51.5 us (0.05); the launches traced: 1040 us -> 51.3 us
  local copies, waits for them, and re-layouts: 869 us -> 4.58 us
  waiting for transfers between devices: 85.1 us -> 0 us
  Pallas kernels: 0 us -> 46 us
  starting transfers between devices: 24 us -> 0 us
  between operations: 19.5 us -> 0.66 us
  blocking collectives: 16.9 us -> 0 us
  other arithmetic: 16.3 us -> 0 us
    gather x370 -> x0, local copies, waits for them, and re-layouts: 848 us -> none  [the longest x360 843 us: apply_operator(): cycle_sum = cycle_sum + buffer[:, stencil[6 * distance + member]]]
    pallas_call x0 -> x1, Pallas kernels: none -> 46 us  [shards(): pl.pallas_call(functools.partial(kernel, D, B, gram), out_shape=(jax.Shap...]
    all_gather x2 -> x0, waiting for transfers between devices: 39.8 us -> none  [the longest x1 39.8 us: shards(): piece_applied = lax.all_gather(applied, 'band', axis=0, tiled=True)]
    unnamed x6 -> x0, waiting for transfers between devices: 38.5 us -> none
    ppermute x10 -> x0, starting transfers between devices: 23.8 us -> none  [the longest x5 16.3 us: with_halo(): lax.ppermute(lax.slice_in_dim(block, block.shape[dim] - width, None, axis...]
    unnamed x614 -> x12, local copies, waits for them, and re-layouts: 18.4 us -> 3.9 us
  transfers between devices with their start and end apart: 14 -> 0, of which waited for: 7 -> 0; matrix products, arithmetic and copies ran while one was open for 17% -> 0% of each run, Pallas kernels for 0% -> 0%
where the time goes in v1:
time: 51.5 us; the launch traced here: 51.3 us
  Pallas kernels  46 us (89%)
  local copies, waits for them, and re-layouts  4.58 us (9%)
  between operations  0.66 us (1%)
    pallas_call x1, Pallas kernels, shards(): pl.pallas_call(functools.partial(kernel, D, B, gram), out_shape=(jax.Shap...  46 us
    unnamed x12, local copies, waits for them, and re-layouts  3.9 us

profile of v1, /device:TPU:0, one launch (start us, length us, event | category | flops | bytes accessed | tf_op | source)
XLA Modules:
  0.0 51.3 jit_solution(13528866991689862738)
XLA Ops:
  0.6 0.0 copy-start.4
  0.6 0.0 copy-start.3
  0.7 0.6 %copy-done.4 = s32[2,1]{0,1:T(1,128)S(1)} copy-done((s32[2,1]{0,1:T(1,128)S(1)}, s32[2,1]{0,1:T(1,128)}, u32[]{:S(2)}) %copy-start.4) | copy-done | bytes 32
  1.3 0.1 copy.8.count_ref
  1.4 0.0 copy-done.3
  1.4 0.0 copy-start
  1.4 0.9 %copy-done = s32[36,1024]{1,0:T(8,128)S(1)} copy-done((s32[36,1024]{1,0:T(8,128)S(1)}, s32[36,1024]{1,0:T(8,128)}, u32[]{:S(2)}) %copy-start) | copy-done | bytes 147480
  2.3 0.0 copy-start.1
  2.3 0.9 %copy-done.1 = f32[32,1024]{1,0:T(8,128)S(1)} copy-done((f32[32,1024]{1,0:T(8,128)S(1)}, f32[32,1024]{1,0:T(8,128)}, u32[]{:S(2)}) %copy-start.1) | copy-done | bytes 131096
  3.2 0.0 copy-start.2
  3.2 0.7 %copy-done.2 = f32[1024]{0:T(1024)S(1)} copy-done((f32[1024]{0:T(1024)S(1)}, f32[1024]{0:T(1024)}, u32[]{:S(2)}) %copy-start.2) | copy-done | bytes 4120
  3.9 46.0 %shard_map.76 = (f32[32,1024]{1,0:T(8,128)S(1)}, f32[32,128]{1,0:T(8,128)S(1)}) custom-call(f32[32,1024]{1,0:T(8,128)S(1)} %copy-done.1, f32[1,1024]{1,0:T(1,128)S(1)} %bitcast.1, s32[36,1024]{1,0:T(8,128)S(1)} %copy-done, s32[2,256]{1,0:T(2,128)S(1)} %copy-done.3, s32[2,1]{1,0:T(2,128)S(1)} %copy.8.count_ref), custom_call_target="tpu_custom_call" | custom-call | tf_op jit(solution)/shard_map/pallas_call | solution.py:344
  49.9 0.7 %fusion = (f32[32,64]{1,0:T(8,128)}, f32[32,64]{1,0:T(8,128)}) fusion(f32[32,128]{1,0:T(8,128)S(1)} %get-tuple-element.6), kind=kLoop, calls=%fused_computation | loop fusion | bytes 32768 | tf_op jit(solution)/shard_map/slice | solution.py:359
  50.6 0.7 %copy.10 = f32[32,1024]{1,0:T(8,128)} copy(f32[32,1024]{1,0:T(8,128)S(1)} %get-tuple-element.12) | data formatting | bytes 262144
Async XLA Ops:
  0.6 0.7 %copy-start.4 = (s32[2,1]{0,1:T(1,128)S(1)}, s32[2,1]{0,1:T(1,128)}, u32[]{:S(2)}) copy-start(s32[2,1]{0,1:T(1,128)} %param.9) | copy-start | bytes 28
  0.6 0.7 %copy-start.3 = (s32[2,256]{1,0:T(2,128)S(1)}, s32[2,256]{1,0:T(2,128)}, u32[]{:S(2)}) copy-start(s32[2,256]{1,0:T(2,128)} %list_ref.1) | copy-start | bytes 6148
  1.4 0.9 %copy-start = (s32[36,1024]{1,0:T(8,128)S(1)}, s32[36,1024]{1,0:T(8,128)}, u32[]{:S(2)}) copy-start(s32[36,1024]{1,0:T(8,128)} %sten_ref.1) | copy-start | bytes 442372
  2.3 0.9 %copy-start.1 = (f32[32,1024]{1,0:T(8,128)S(1)}, f32[32,1024]{1,0:T(8,128)}, u32[]{:S(2)}) copy-start(f32[32,1024]{1,0:T(8,128)} %orb_ref.1) | copy-start | bytes 393220
  3.2 0.7 %copy-start.2 = (f32[1024]{0:T(1024)S(1)}, f32[1024]{0:T(1024)}, u32[]{:S(2)}) copy-start(f32[1024]{0:T(1024)} %param.6) | copy-start | bytes 12292

commit v2 on v1

--- a/solution.py
+++ b/solution.py
@@ -48,8 +48,18 @@
     return both[:hi_rows] + both[hi_rows:] + low
 
 
-def kernel(D, B, gram, orb_ref, pot_ref, sten_ref, list_ref, count_ref, filt_ref, out_ref, *scratch):
+def kernel(D, B, gram, orb_in, pot_in, sten_in, list_in, count_ref, filt_ref, out_ref, *scratch):
+    orb_ref, pot_ref, sten_ref, list_ref, in_sem = scratch[:5]
+    scratch = scratch[5:]
     ah, al, sel, slot, unit, mm, sent, halo, mm_ss, mm_rs, h_ss, h_rs = scratch[:12]
+    fetches = [
+        pltpu.make_async_copy(source, target, in_sem.at[n])
+        for n, (source, target) in enumerate(
+            ((list_in, list_ref), (pot_in, pot_ref), (orb_in, orb_ref), (sten_in, sten_ref))
+        )
+    ]
+    for fetch in fetches:
+        fetch.start()
     d = lax.axis_index("domain")
     b = lax.axis_index("band")
     R, N = orb_ref.shape
@@ -68,6 +78,8 @@
                 barrier, inc=1, device_id={"band": lax.rem(b + o, B)}, device_id_type=MESH
             )
 
+    for fetch in fetches[:2]:
+        fetch.wait()
     pot = pot_ref[...]
     mm[0, 0:1] = jnp.broadcast_to(jnp.min(pot, axis=1, keepdims=True), (1, 128))
     mm[0, 1:2] = jnp.broadcast_to(jnp.max(pot, axis=1, keepdims=True), (1, 128))
@@ -123,9 +135,11 @@
         pl.when(d < D - 1)(upward.wait_send)
         pl.when(d > 0)(downward.wait_send)
 
+    fetches[2].wait()
     first = jnp.concatenate(split(orb_ref[...]), axis=0)
     send_halo(0, first)
 
+    fetches[3].wait()
     key = sten_ref[...]
     digit = (key * ((1 << 22) // groups + 1)) >> 22
     slot[...] = key - digit * groups
@@ -196,8 +210,8 @@
             done_halo(step)
         return
 
-    app, fall, aall, give, core_in, y_in, band_out, band_in = scratch[12:20]
-    f_ss, f_rs, a_ss, a_rs, c_ss, c_rs, y_ss, y_rs, b_ss, b_rs = scratch[20:]
+    app, fall, aall, give, keep, core_in, y_in, band_out, band_in = scratch[12:21]
+    f_ss, f_rs, a_ss, a_rs, c_ss, c_rs, y_ss, y_rs, b_ss, b_rs = scratch[21:]
     wide = N // B
 
     def spread(src, dst, ss, rs):
@@ -248,46 +262,74 @@
         return both[:orbs] + both[orbs:] + low
 
     pairs = D // 2
+    chunks = D
+    per = B // chunks
+    height = per * R
+    order = [lax.rem(b // per + 1 + i, chunks) for i in range(chunks)]
+    spans = [pl.ds(pl.multiple_of(h * height, height), height) for h in order]
     c_copies = []
     for q in range(pairs):
         turn = lax.rem(pair + 1 + q, pairs)
         give[q] = partial(2 * turn + (1 - core))
-        copy = remote(
-            give.at[q], core_in.at[q], c_ss.at[q], c_rs.at[q], {"domain": 2 * pair + 1 - core}
-        )
-        copy.start()
-        c_copies.append(copy)
-    y_copies = []
-    for q in range(pairs):
-        turn = lax.rem(pair + 1 + q, pairs)
-        own = partial(2 * turn + core)
-        c_copies[q].wait_recv()
-        core_in[q] = core_in[q] + own
-        if q < pairs - 1:
+        row = []
+        for i in range(chunks):
             copy = remote(
-                core_in.at[q], y_in.at[q], y_ss.at[q], y_rs.at[q], {"domain": 2 * turn + core}
+                give.at[q, spans[i]],
+                core_in.at[q, spans[i]],
+                c_ss.at[q, i],
+                c_rs.at[q, i],
+                {"domain": 2 * pair + 1 - core},
             )
             copy.start()
-            y_copies.append(copy)
-    total = core_in[pairs - 1]
+            row.append(copy)
+        c_copies.append(row)
+    for q in range(pairs):
+        keep[q] = partial(2 * lax.rem(pair + 1 + q, pairs) + core)
+    y_copies = []
     for q in range(pairs - 1):
-        y_copies[q].wait_recv()
-        total = total + y_in[q]
-    band_out[...] = (total * (1.0 / (N * D))).reshape(band_out.shape)
-    b_copies = []
-    for o in range(1, B):
-        to = lax.rem(b + o, B)
-        copy = remote(band_out.at[to], band_in.at[o - 1], b_ss.at[o - 1], b_rs.at[o - 1], {"band": to})
-        copy.start()
-        b_copies.append(copy)
+        turn = lax.rem(pair + 1 + q, pairs)
+        row = []
+        for i in range(chunks):
+            c_copies[q][i].wait_recv()
+            keep[q, spans[i]] = keep[q, spans[i]] + core_in[q, spans[i]]
+            copy = remote(
+                keep.at[q, spans[i]],
+                y_in.at[q, spans[i]],
+                y_ss.at[q, i],
+                y_rs.at[q, i],
+                {"domain": 2 * turn + core},
+            )
+            copy.start()
+            row.append(copy)
+        y_copies.append(row)
+
+    def band_copy(to):
+        return remote(band_out.at[to], band_in.at[b], b_ss.at[to], b_rs.at[b], {"band": to})
+
+    for i in range(chunks):
+        c_copies[pairs - 1][i].wait_recv()
+        total = keep[pairs - 1, spans[i]] + core_in[pairs - 1, spans[i]]
+        for q in range(pairs - 1):
+            y_copies[q][i].wait_recv()
+            total = total + y_in[q, spans[i]]
+        total = total * (1.0 / (N * D))
+        for t in range(per):
+            to = order[i] * per + t
+            band_out[to] = total[t * R : (t + 1) * R]
+            pl.when(to != b)(band_copy(to).start)
     result = band_out[b]
     for o in range(1, B):
-        b_copies[o - 1].wait_recv()
-        result = result + band_in[o - 1]
+        other = lax.rem(b + o, B)
+        remote(
+            band_out.at[other], band_in.at[other], b_ss.at[other], b_rs.at[other], {"band": other}
+        ).wait_recv()
+        result = result + band_in[other]
     out_ref[...] = result
+    for o in range(1, B):
+        band_copy(lax.rem(b + o, B)).wait_send()
     for step in range(DEGREE + 1):
         done_halo(step)
-    for copy in f_copies + a_copies + c_copies + y_copies + b_copies:
+    for copy in f_copies + a_copies + sum(c_copies + y_copies, []):
         copy.wait_send()
 
 
@@ -311,6 +353,11 @@
     steps = DEGREE + 1
     dma = pltpu.SemaphoreType.DMA
     scratch = [
+        pltpu.VMEM((R, N), f32),
+        pltpu.VMEM((1, N), f32),
+        pltpu.VMEM(stencil.shape, i32),
+        pltpu.VMEM(send_list.shape, i32),
+        dma((4,)),
         pltpu.VMEM((keys, N), bf16),
         pltpu.VMEM((keys, N), bf16),
         pltpu.VMEM((N, 2 * cap), bf16),
@@ -334,12 +381,13 @@
             pltpu.VMEM((B, R, wide), f32),
             pltpu.VMEM((pairs, orbs, width), f32),
             pltpu.VMEM((pairs, orbs, width), f32),
+            pltpu.VMEM((pairs, orbs, width), f32),
             pltpu.VMEM((pairs - 1, orbs, width), f32),
             pltpu.VMEM((B, R, width), f32),
-            pltpu.VMEM((B - 1, R, width), f32),
+            pltpu.VMEM((B, R, width), f32),
         ]
-        for count in (B - 1, B - 1, pairs, pairs - 1, B - 1):
-            scratch += [dma((count,)), dma((count,))]
+        for counts in ((B - 1,), (B - 1,), (pairs, D), (pairs - 1, D), (B,)):
+            scratch += [dma(counts), dma(counts)]
     second = (R, 2 * orbs // D) if gram else (R, N)
     filtered, other = pl.pallas_call(
         functools.partial(kernel, D, B, gram),
@@ -347,7 +395,8 @@
             jax.ShapeDtypeStruct((R, N), f32),
             jax.ShapeDtypeStruct(second, f32),
         ),
-        in_specs=[pl.BlockSpec(memory_space=pltpu.VMEM)] * 5,
+        in_specs=[pl.BlockSpec(memory_space=pl.ANY)] * 4
+        + [pl.BlockSpec(memory_space=pltpu.VMEM)],
         out_specs=[pl.BlockSpec(memory_space=pltpu.VMEM)] * 2,
         scratch_shapes=scratch,
         compiler_params=pltpu.CompilerParams(

time: 51.5 us -> 50.6 us (0.983)
  Pallas kernels: 46 us -> 45.2 us
    pallas_call x1, Pallas kernels: 46 us -> 45.2 us  [shards(): pl.pallas_call(functools.partial(kernel, D, B, gram), out_shape=(jax.Shap...]
where the time goes in v2:
time: 50.6 us; the launch traced here: 50.4 us
  Pallas kernels  45.2 us (89%)
  local copies, waits for them, and re-layouts  4.58 us (9%)
  between operations  0.66 us (1%)
    pallas_call x1, Pallas kernels, shards(): pl.pallas_call(functools.partial(kernel, D, B, gram), out_shape=(jax.Shap...  45.2 us
    unnamed x12, local copies, waits for them, and re-layouts  3.9 us

profile of v2, /device:TPU:0, one launch (start us, length us, event | category | flops | bytes accessed | tf_op | source)
XLA Modules:
  0.0 50.4 jit_solution(1685560656887002587)
XLA Ops:
  0.6 0.0 copy-start.4
  0.6 0.0 copy-start.3
  0.7 0.6 %copy-done.4 = s32[2,1]{0,1:T(1,128)S(1)} copy-done((s32[2,1]{0,1:T(1,128)S(1)}, s32[2,1]{0,1:T(1,128)}, u32[]{:S(2)}) %copy-start.4) | copy-done | bytes 32
  1.3 0.1 copy.8.count_ref
  1.4 0.0 copy-done.3
  1.4 0.0 copy-start
  1.4 0.9 %copy-done = s32[36,1024]{1,0:T(8,128)S(1)} copy-done((s32[36,1024]{1,0:T(8,128)S(1)}, s32[36,1024]{1,0:T(8,128)}, u32[]{:S(2)}) %copy-start) | copy-done | bytes 147480
  2.3 0.0 copy-start.1
  2.3 0.9 %copy-done.1 = f32[32,1024]{1,0:T(8,128)S(1)} copy-done((f32[32,1024]{1,0:T(8,128)S(1)}, f32[32,1024]{1,0:T(8,128)}, u32[]{:S(2)}) %copy-start.1) | copy-done | bytes 131096
  3.2 0.0 copy-start.2
  3.2 0.7 %copy-done.2 = f32[1024]{0:T(1024)S(1)} copy-done((f32[1024]{0:T(1024)S(1)}, f32[1024]{0:T(1024)}, u32[]{:S(2)}) %copy-start.2) | copy-done | bytes 4120
  3.9 45.2 %shard_map.76 = (f32[32,1024]{1,0:T(8,128)S(1)}, f32[32,128]{1,0:T(8,128)S(1)}) custom-call(f32[32,1024]{1,0:T(8,128)S(1)} %copy-done.1, f32[1,1024]{1,0:T(1,128)S(1)} %bitcast.1, s32[36,1024]{1,0:T(8,128)S(1)} %copy-done, s32[2,256]{1,0:T(2,128)S(1)} %copy-done.3, s32[2,1]{1,0:T(2,128)S(1)} %copy.8.count_ref), custom_call_target="tpu_custom_call" | custom-call | tf_op jit(solution)/shard_map/pallas_call | solution.py:392
  49.1 0.7 %fusion = (f32[32,64]{1,0:T(8,128)}, f32[32,64]{1,0:T(8,128)}) fusion(f32[32,128]{1,0:T(8,128)S(1)} %get-tuple-element.6), kind=kLoop, calls=%fused_computation | loop fusion | bytes 32768 | tf_op jit(solution)/shard_map/slice | solution.py:408
  49.8 0.7 %copy.10 = f32[32,1024]{1,0:T(8,128)} copy(f32[32,1024]{1,0:T(8,128)S(1)} %get-tuple-element.12) | data formatting | bytes 262144
Async XLA Ops:
  0.6 0.7 %copy-start.4 = (s32[2,1]{0,1:T(1,128)S(1)}, s32[2,1]{0,1:T(1,128)}, u32[]{:S(2)}) copy-start(s32[2,1]{0,1:T(1,128)} %param.9) | copy-start | bytes 28
  0.6 0.7 %copy-start.3 = (s32[2,256]{1,0:T(2,128)S(1)}, s32[2,256]{1,0:T(2,128)}, u32[]{:S(2)}) copy-start(s32[2,256]{1,0:T(2,128)} %list_in.1) | copy-start | bytes 6148
  1.4 0.9 %copy-start = (s32[36,1024]{1,0:T(8,128)S(1)}, s32[36,1024]{1,0:T(8,128)}, u32[]{:S(2)}) copy-start(s32[36,1024]{1,0:T(8,128)} %sten_in.1) | copy-start | bytes 442372
  2.3 0.9 %copy-start.1 = (f32[32,1024]{1,0:T(8,128)S(1)}, f32[32,1024]{1,0:T(8,128)}, u32[]{:S(2)}) copy-start(f32[32,1024]{1,0:T(8,128)} %orb_in.1) | copy-start | bytes 393220
  3.2 0.7 %copy-start.2 = (f32[1024]{0:T(1024)S(1)}, f32[1024]{0:T(1024)}, u32[]{:S(2)}) copy-start(f32[1024]{0:T(1024)} %param.6) | copy-start | bytes 12292

commit v3 on v2

--- a/solution.py
+++ b/solution.py
@@ -395,12 +395,12 @@
             jax.ShapeDtypeStruct((R, N), f32),
             jax.ShapeDtypeStruct(second, f32),
         ),
-        in_specs=[pl.BlockSpec(memory_space=pl.ANY)] * 4
+        in_specs=[pl.BlockSpec(memory_space=pltpu.HBM)] * 4
         + [pl.BlockSpec(memory_space=pltpu.VMEM)],
         out_specs=[pl.BlockSpec(memory_space=pltpu.VMEM)] * 2,
         scratch_shapes=scratch,
         compiler_params=pltpu.CompilerParams(
-            collective_id=0, has_side_effects=True, vmem_limit_bytes=48 * 1024 * 1024
+            collective_id=0, has_side_effects=True, vmem_limit_bytes=56 * 1024 * 1024
         ),
     )(orbitals, potential.reshape(1, N), stencil, send_list, send_count)
     if gram:

time: 50.6 us -> 51.5 us (1.018)
  Pallas kernels: 45.2 us -> 46.2 us
    unnamed x12 -> x4, local copies, waits for them, and re-layouts: 3.9 us -> 2.86 us
    pallas_call x1, Pallas kernels: 45.2 us -> 46.2 us  [shards(): pl.pallas_call(functools.partial(kernel, D, B, gram), out_shape=(jax.Shap...]
    slice x1, local copies, waits for them, and re-layouts: 0.68 us -> 1.47 us  [shards(): return (filtered, other[:, :half], other[:, half:])]
where the time goes in v3:
time: 51.5 us; the launch traced here: 51.1 us
  Pallas kernels  46.2 us (90%)
  local copies, waits for them, and re-layouts  4.34 us (8%)
  between operations  0.65 us (1%)
    pallas_call x1, Pallas kernels, shards(): pl.pallas_call(functools.partial(kernel, D, B, gram), out_shape=(jax.Shap...  46.2 us
    unnamed x4, local copies, waits for them, and re-layouts  2.86 us
    slice x1, local copies, waits for them, and re-layouts, shards(): return (filtered, other[:, :half], other[:, half:])  1.47 us

profile of v3, /device:TPU:0, one launch (start us, length us, event | category | flops | bytes accessed | tf_op | source)
XLA Modules:
  0.0 51.1 jit_solution(15155284660200652683)
XLA Ops:
  0.6 0.0 copy-start
  0.6 0.6 %copy-done = s32[2,1]{0,1:T(1,128)S(1)} copy-done((s32[2,1]{0,1:T(1,128)S(1)}, s32[2,1]{0,1:T(1,128)}, u32[]{:S(2)}) %copy-start) | copy-done | bytes 32
  1.3 0.6 %copy.8.count_ref = s32[2,1]{1,0:T(2,128)} copy(s32[2,1]{0,1:T(1,128)S(1)} %copy-done) | data formatting | bytes 16 | tf_op args[4]
  1.9 46.2 %shard_map.76 = (f32[32,1024]{1,0:T(8,128)}, f32[32,128]{1,0:T(8,128)}) custom-call(f32[32,1024]{1,0:T(8,128)} %orb_in.1, f32[1,1024]{1,0:T(1,128)} %bitcast.1, s32[36,1024]{1,0:T(8,128)} %sten_in.1, s32[2,256]{1,0:T(2,128)} %list_in.1, s32[2,1]{1,0:T(2,128)} %copy.8.count_ref), custom_call_target="tpu_custom_call" | custom-call | tf_op jit(solution)/shard_map/pallas_call | solution.py:392
  48.1 1.5 %fusion = (f32[32,64]{1,0:T(8,128)}, f32[32,64]{1,0:T(8,128)}) fusion(f32[32,128]{1,0:T(8,128)} %get-tuple-element.6), kind=kLoop, calls=%fused_computation | loop fusion | bytes 32768 | tf_op jit(solution)/shard_map/slice | solution.py:408
  49.6 1.6 %copy.10 = f32[32,1024]{1,0:T(8,128)} copy(f32[32,1024]{1,0:T(8,128)} %get-tuple-element.12) | data formatting | bytes 262144
Async XLA Ops:
  0.6 0.7 %copy-start = (s32[2,1]{0,1:T(1,128)S(1)}, s32[2,1]{0,1:T(1,128)}, u32[]{:S(2)}) copy-start(s32[2,1]{0,1:T(1,128)} %param.9) | copy-start | bytes 28

commit v4 on v3

--- a/solution.py
+++ b/solution.py
@@ -400,7 +400,7 @@
         out_specs=[pl.BlockSpec(memory_space=pltpu.VMEM)] * 2,
         scratch_shapes=scratch,
         compiler_params=pltpu.CompilerParams(
-            collective_id=0, has_side_effects=True, vmem_limit_bytes=56 * 1024 * 1024
+            collective_id=0, has_side_effects=True, vmem_limit_bytes=48 * 1024 * 1024
         ),
     )(orbitals, potential.reshape(1, N), stencil, send_list, send_count)
     if gram:

time: 51.5 us -> 50.6 us (0.983)
  Pallas kernels: 46.2 us -> 45.2 us
    unnamed x4 -> x12, local copies, waits for them, and re-layouts: 2.86 us -> 3.9 us
    pallas_call x1, Pallas kernels: 46.2 us -> 45.2 us  [shards(): pl.pallas_call(functools.partial(kernel, D, B, gram), out_shape=(jax.Shap...]
    slice x1, local copies, waits for them, and re-layouts: 1.47 us -> 0.68 us  [shards(): return (filtered, other[:, :half], other[:, half:])]
where the time goes in v4:
time: 50.6 us; the launch traced here: 50.4 us
  Pallas kernels  45.2 us (89%)
  local copies, waits for them, and re-layouts  4.58 us (9%)
  between operations  0.66 us (1%)
    pallas_call x1, Pallas kernels, shards(): pl.pallas_call(functools.partial(kernel, D, B, gram), out_shape=(jax.Shap...  45.2 us
    unnamed x12, local copies, waits for them, and re-layouts  3.9 us

profile of v4, /device:TPU:0, one launch (start us, length us, event | category | flops | bytes accessed | tf_op | source)
XLA Modules:
  0.0 50.4 jit_solution(1685560656887002587)
XLA Ops:
  0.6 0.0 copy-start.4
  0.6 0.0 copy-start.3
  0.7 0.6 %copy-done.4 = s32[2,1]{0,1:T(1,128)S(1)} copy-done((s32[2,1]{0,1:T(1,128)S(1)}, s32[2,1]{0,1:T(1,128)}, u32[]{:S(2)}) %copy-start.4) | copy-done | bytes 32
  1.3 0.1 copy.8.count_ref
  1.4 0.0 copy-done.3
  1.4 0.0 copy-start
  1.4 0.9 %copy-done = s32[36,1024]{1,0:T(8,128)S(1)} copy-done((s32[36,1024]{1,0:T(8,128)S(1)}, s32[36,1024]{1,0:T(8,128)}, u32[]{:S(2)}) %copy-start) | copy-done | bytes 147480
  2.3 0.0 copy-start.1
  2.3 0.9 %copy-done.1 = f32[32,1024]{1,0:T(8,128)S(1)} copy-done((f32[32,1024]{1,0:T(8,128)S(1)}, f32[32,1024]{1,0:T(8,128)}, u32[]{:S(2)}) %copy-start.1) | copy-done | bytes 131096
  3.2 0.0 copy-start.2
  3.2 0.7 %copy-done.2 = f32[1024]{0:T(1024)S(1)} copy-done((f32[1024]{0:T(1024)S(1)}, f32[1024]{0:T(1024)}, u32[]{:S(2)}) %copy-start.2) | copy-done | bytes 4120
  3.9 45.2 %shard_map.76 = (f32[32,1024]{1,0:T(8,128)S(1)}, f32[32,128]{1,0:T(8,128)S(1)}) custom-call(f32[32,1024]{1,0:T(8,128)S(1)} %copy-done.1, f32[1,1024]{1,0:T(1,128)S(1)} %bitcast.1, s32[36,1024]{1,0:T(8,128)S(1)} %copy-done, s32[2,256]{1,0:T(2,128)S(1)} %copy-done.3, s32[2,1]{1,0:T(2,128)S(1)} %copy.8.count_ref), custom_call_target="tpu_custom_call" | custom-call | tf_op jit(solution)/shard_map/pallas_call | solution.py:392
  49.1 0.7 %fusion = (f32[32,64]{1,0:T(8,128)}, f32[32,64]{1,0:T(8,128)}) fusion(f32[32,128]{1,0:T(8,128)S(1)} %get-tuple-element.6), kind=kLoop, calls=%fused_computation | loop fusion | bytes 32768 | tf_op jit(solution)/shard_map/slice | solution.py:408
  49.8 0.7 %copy.10 = f32[32,1024]{1,0:T(8,128)} copy(f32[32,1024]{1,0:T(8,128)S(1)} %get-tuple-element.12) | data formatting | bytes 262144
Async XLA Ops:
  0.6 0.7 %copy-start.4 = (s32[2,1]{0,1:T(1,128)S(1)}, s32[2,1]{0,1:T(1,128)}, u32[]{:S(2)}) copy-start(s32[2,1]{0,1:T(1,128)} %param.9) | copy-start | bytes 28
  0.6 0.7 %copy-start.3 = (s32[2,256]{1,0:T(2,128)S(1)}, s32[2,256]{1,0:T(2,128)}, u32[]{:S(2)}) copy-start(s32[2,256]{1,0:T(2,128)} %list_in.1) | copy-start | bytes 6148
  1.4 0.9 %copy-start = (s32[36,1024]{1,0:T(8,128)S(1)}, s32[36,1024]{1,0:T(8,128)}, u32[]{:S(2)}) copy-start(s32[36,1024]{1,0:T(8,128)} %sten_in.1) | copy-start | bytes 442372
  2.3 0.9 %copy-start.1 = (f32[32,1024]{1,0:T(8,128)S(1)}, f32[32,1024]{1,0:T(8,128)}, u32[]{:S(2)}) copy-start(f32[32,1024]{1,0:T(8,128)} %orb_in.1) | copy-start | bytes 393220
  3.2 0.7 %copy-start.2 = (f32[1024]{0:T(1024)S(1)}, f32[1024]{0:T(1024)}, u32[]{:S(2)}) copy-start(f32[1024]{0:T(1024)} %param.6) | copy-start | bytes 12292
